TPU v7x, 32 devices: a whole 2x2x4 slice. The times are simulated.
32 devices in a mesh: prod: 8 (over z, y), hid: 4 (over x, core).
Axes of the slice: x: 2, y: 2, z: 4, core: 2. Of those that a mesh axis runs over, the one named last changes fastest.
Arguments:
- fingerprints: bfloat16 [8192, 16384], P('prod'), may hold values from 0 to 3
- w_first: bfloat16 [16384, 2048], P(None, 'hid'), may hold values from -0.046875 to 0.046875
- b_first: float32 [2048], P('hid'), may hold values from -4 to 4
- w_second: bfloat16 [2048, 1024], replicated, may hold values from -0.125 to 0.125
- b_second: float32 [1024], replicated, may hold values from -4 to 4
- w_third: float32 [1024], replicated, may hold values from -0.1875 to 0.1875
- synth_block: int32 [16384, 3], P('prod'), may hold values from 0 to 7
- synth_row: int32 [16384, 3], P('prod'), may hold values from 0 to 1023
- third_used: int32 [16384], P('prod'), may hold values 0 or 1
Outputs:
- score: float32 [16384], P(('prod', 'hid'))
Inputs may be any that keep to these rules, and one draw needn't show every extreme that they name: `synth_row`: rows within a block.
All inputs are finite; a program needn't handle non-finite values. No bound on the sum of `third_used` on one device may be relied on, other than what follows from the above.
Results may differ from a plain program's by a relative error of at most 0.0083.
Values may be sent and summed in bfloat16 or wider, within the bound.
A program may use at most 384 MiB of HBM per device.

v0:
```python
import jax
import jax.numpy as jnp
from jax import lax
from jax.sharding import PartitionSpec as P


def gelu_tanh(value):
    return (
        0.5
        * value
        * (1.0 + jnp.tanh(0.7978845608028654 * (value + 0.044715 * value * value * value)))
    )


def local(
    fingerprints, w_first, b_first, w_second, b_second, w_third, synth_block, synth_row, third_used
):
    syn_rows = fingerprints.shape[0]
    prod_rows = synth_block.shape[0]
    units = w_first.shape[1]
    synth_hidden = jnp.dot(fingerprints, w_first, preferred_element_type=jnp.float32).astype(
        jnp.bfloat16
    )
    glob = synth_block * syn_rows + synth_row
    ones_col = jnp.ones((prod_rows, 1), jnp.int32)
    live = jnp.concatenate([ones_col, ones_col, third_used[:, None]], axis=1)
    piece = lax.all_gather(synth_hidden, "prod", axis=0, tiled=True)
    columns = lax.iota(jnp.int32, piece.shape[0])
    hits = jnp.where(glob[:, :, None] == columns[None, None, :], live[:, :, None], 0)
    select = jnp.sum(hits, axis=1).astype(jnp.bfloat16)
    composed = jnp.dot(select, piece, preferred_element_type=jnp.float32)
    act = gelu_tanh(composed + b_first[None, :]).astype(jnp.bfloat16)
    my_rows = lax.dynamic_slice_in_dim(w_second, lax.axis_index("hid") * units, units, 0)
    second = lax.psum_scatter(
        jnp.dot(act, my_rows, preferred_element_type=jnp.float32),
        "hid",
        scatter_dimension=0,
        tiled=True,
    )
    out = gelu_tanh(second + b_second[None, :])
    return jnp.sum(out * w_third[None, :], axis=1)


def solution(mesh):
    placed = (
        P("prod", None),
        P(None, "hid"),
        P("hid"),
        P(),
        P(),
        P(),
        P("prod", None),
        P("prod", None),
        P("prod"),
    )
    return jax.shard_map(
        local, mesh=mesh, in_specs=placed, out_specs=P(("prod", "hid")), check_vma=False
    )
```

profile of v0, /device:TPU:0, one launch (start us, length us, event | category | flops | bytes accessed | tf_op | source)
XLA Modules:
  0.0 272.7 jit_solution(4516989337029554333)
XLA Ops:
  6.5 0.0 copy-start.2
  6.5 0.0 copy-start
  6.5 0.0 copy-start.1
  6.5 0.0 all-gather.2.cloned.1.call-start
  6.5 25.4 %convolution_convert_fusion = bf16[1024,512]{1,0:T(8,128)(2,1)} fusion(bf16[1024,16384]{1,0:T(8,128)(2,1)} %param.9, bf16[16384,512]{1,0:T(8,128)(2,1)} %param.10), kind=kOutput, calls=%fused_computation.17 | convolution fusion | flops 17180393472 | bytes 51380224 | tf_op jit(solution)/shard_map/dot_general | solution.py:21
  32.0 0.0 all-gather.2.cloned.1.call-update
  32.0 0.0 reduce-scatter.2.cloned.1.call-start
  32.0 0.0 copy-done.2
  32.1 0.0 copy-done
  32.1 0.0 copy-done.1
  32.1 0.0 copy-start.5
  32.1 56.2 %select_reduce_fusion = s32[2048,8192]{1,0:T(8,128)} fusion(s32[2048,3]{0,1:T(4,128)S(1)} %concatenate.4, s32[2048,3]{0,1:T(4,128)S(1)} %multiply_add_fusion.2), kind=kLoop, calls=%fused_computation | loop fusion | flops 134217728 | bytes 67158016 | tf_op jit(solution)/shard_map/reduce_sum | solution.py:30
  88.3 71.8 %all-gather.2.cloned.1.call-done = bf16[8192,512]{1,0:T(8,128)(2,1)} async-done(((bf16[1024,512]{1,0:T(8,128)(2,1)}), bf16[8192,512]{1,0:T(8,128)(2,1)}) %all-gather.2.cloned.1.call-update) | async-done | bytes 8388624 | tf_op jit(solution)/shard_map/all_gather | solution.py:27
  160.1 0.0 copy-done.5
  160.1 32.6 %fusion.15 = f32[2048,1024]{1,0:T(8,128)} fusion(bf16[2048,1024]{1,0:T(8,128)(2,1)} %param.12, s32[]{:T(128)S(6)} %select_n.8, bf16[8192,512]{1,0:T(8,128)(2,1)} %all-gather.2.cloned.1.call-done, s32[2048,8192]{1,0:T(8,128)} %select_reduce_fusion, f32[512]{0:T(512)S(1)} %copy-done.5), kind=kOutput, calls=%fused_computation.18 | convolution fusion | flops 19354615808 | bytes 84936704 | tf_op jit(solution)/shard_map/dot_general | solution.py:35
  192.7 0.0 copy-start.3
  192.7 0.0 copy-start.4
  192.7 0.0 reduce-scatter.2.cloned.1.call-update
  192.7 70.1 %reduce-scatter.2.cloned.1.call-done = f32[512,1024]{1,0:T(8,128)} async-done(((f32[2048,1024]{1,0:T(8,128)}), f32[512,1024]{1,0:T(8,128)}) %reduce-scatter.2.cloned.1.call-update) | async-done | bytes 2097168 | tf_op jit(solution)/shard_map/reduce_scatter | solution.py:34
  262.7 0.0 copy-done.3
  262.8 0.0 copy-done.4
  262.8 3.1 %fusion.14 = f32[512]{0:T(512)} fusion(f32[512,1024]{1,0:T(8,128)} %reduce-scatter.2.cloned.1.call-done, f32[1024]{0:T(1024)S(1)} %copy-done.3, f32[1024]{0:T(1024)S(1)} %copy-done.4), kind=kLoop, calls=%fused_computation.16 | loop fusion | flops 5766656 | bytes 2107392 | tf_op jit(solution)/shard_map/reduce_sum | solution.py:41
  (2 shorter events, 0.0 us)
Async XLA Ops:
  6.5 25.5 %copy-start.2 = (s32[2048]{0:T(1024)S(1)}, s32[2048]{0:T(1024)}, u32[]{:S(2)}) copy-start(s32[2048]{0:T(1024)} %param.17) | copy-start | bytes 24580
  6.5 25.5 %copy-start = (s32[2048,3]{0,1:T(4,128)S(1)}, s32[2048,3]{0,1:T(4,128)}, u32[]{:S(2)}) copy-start(s32[2048,3]{0,1:T(4,128)} %param.16) | copy-start | bytes 73732
  6.5 25.5 %copy-start.1 = (s32[2048,3]{0,1:T(4,128)S(1)}, s32[2048,3]{0,1:T(4,128)}, u32[]{:S(2)}) copy-start(s32[2048,3]{0,1:T(4,128)} %param.15) | copy-start | bytes 73732
  6.5 153.5 %all-gather.2.cloned.1.call-start = ((), (), s32[]{:S(2)}) async-start(), calls=%async_computation.1 | async-start | bytes 9437184 | tf_op jit(solution)/shard_map/all_gather | solution.py:27
  32.0 230.8 %reduce-scatter.2.cloned.1.call-start = ((), (), s32[]{:S(2)}) async-start(), calls=%async_computation.2 | async-start | bytes 10485760 | tf_op jit(solution)/shard_map/reduce_scatter | solution.py:34
  32.1 128.0 %copy-start.5 = (f32[512]{0:T(512)S(1)}, f32[512]{0:T(512)}, u32[]{:S(2)}) copy-start(f32[512]{0:T(512)} %param.11) | copy-start | bytes 6148
  192.7 70.1 %copy-start.3 = (f32[1024]{0:T(1024)S(1)}, f32[1024]{0:T(1024)}, u32[]{:S(2)}) copy-start(f32[1024]{0:T(1024)} %param.14) | copy-start | bytes 12292
  192.7 70.1 %copy-start.4 = (f32[1024]{0:T(1024)S(1)}, f32[1024]{0:T(1024)}, u32[]{:S(2)}) copy-start(f32[1024]{0:T(1024)} %param.13) | copy-start | bytes 12292
Sparse Core Ops, SparseCore 0:
  32.1 127.9 all-gather.1
  192.8 69.8 reduce-scatter.1
where the time goes:
time: 273 us
  waiting for transfers between devices  142 us (52%)
  other arithmetic  59.3 us (22%)
  matrix products  58 us (21%)
  between operations  13.5 us (5%)
    all_gather x1, waiting for transfers between devices, local(): piece = lax.all_gather(synth_hidden, 'prod', axis=0, tiled=True)  71.8 us
    reduce_scatter x1, waiting for transfers between devices, local(): lax.psum_scatter(jnp.dot(act, my_rows, preferred_element_type=jnp.float32...  70.1 us
    reduce_sum x1, other arithmetic, local(): select = jnp.sum(hits, axis=1).astype(jnp.bfloat16)  56.2 us
    dot_general x1, matrix products, local(): jnp.dot(act, my_rows, preferred_element_type=jnp.float32)  32.6 us
    dot_general x1, matrix products, local(): jnp.dot(fingerprints, w_first, preferred_element_type=jnp.float32)  25.4 us
  transfers between devices with their start and end apart: 2, of which 2 were waited for; matrix products, arithmetic and copies ran while one was open for 21% of the time, Pallas kernels for 0%

commit v1 on v0

--- a/solution.py
+++ b/solution.py
@@ -17,7 +17,6 @@
 ):
     syn_rows = fingerprints.shape[0]
     prod_rows = synth_block.shape[0]
-    units = w_first.shape[1]
     synth_hidden = jnp.dot(fingerprints, w_first, preferred_element_type=jnp.float32).astype(
         jnp.bfloat16
     )
@@ -30,13 +29,8 @@
     select = jnp.sum(hits, axis=1).astype(jnp.bfloat16)
     composed = jnp.dot(select, piece, preferred_element_type=jnp.float32)
     act = gelu_tanh(composed + b_first[None, :]).astype(jnp.bfloat16)
-    my_rows = lax.dynamic_slice_in_dim(w_second, lax.axis_index("hid") * units, units, 0)
-    second = lax.psum_scatter(
-        jnp.dot(act, my_rows, preferred_element_type=jnp.float32),
-        "hid",
-        scatter_dimension=0,
-        tiled=True,
-    )
+    traded = lax.all_to_all(act, "hid", split_axis=0, concat_axis=1, tiled=True)
+    second = jnp.dot(traded, w_second, preferred_element_type=jnp.float32)
     out = gelu_tanh(second + b_second[None, :])
     return jnp.sum(out * w_third[None, :], axis=1)
 

time: 273 us -> 232 us (0.85)
  waiting for transfers between devices: 142 us -> 72 us
  blocking collectives: 0 us -> 28.5 us
  other arithmetic: 59.3 us -> 56.2 us
  local copies, waits for them, and re-layouts: 0.04 us -> 2.86 us
    reduce_scatter x1 -> x0, waiting for transfers between devices: 70.1 us -> none  [local(): lax.psum_scatter(jnp.dot(act, my_rows, preferred_element_type=jnp.float32...]
    all_to_all x0 -> x1, blocking collectives: none -> 28.5 us  [local(): traded = lax.all_to_all(act, 'hid', split_axis=0, concat_axis=1, tiled=True)]
    reduce_sum x1 -> x0, other arithmetic: 3.06 us -> none  [local(): return jnp.sum(out * w_third[None, :], axis=1)]
    all_to_all x0 -> x1, local copies, waits for them, and re-layouts: none -> 2.81 us  [local(): traded = lax.all_to_all(act, 'hid', split_axis=0, concat_axis=1, tiled=True)]
    dot_general x1 -> x2, matrix products: 32.6 us -> 33.1 us  [the longest x1 29.6 us: local(): composed = jnp.dot(select, piece, preferred_element_type=jnp.float32)]
  transfers between devices with their start and end apart: 2 -> 1, of which waited for: 2 -> 1; matrix products, arithmetic and copies ran while one was open for 21% -> 24% of each run, Pallas kernels for 0% -> 0%
where the time goes in v1:
time: 232 us; the launch traced here: 231 us
  waiting for transfers between devices  72 us (31%)
  matrix products  58.5 us (25%)
  other arithmetic  56.2 us (24%)
  blocking collectives  28.5 us (12%)
  between operations  13.5 us (6%)
  local copies, waits for them, and re-layouts  2.86 us (1%)
    all_gather x1, waiting for transfers between devices, local(): piece = lax.all_gather(synth_hidden, 'prod', axis=0, tiled=True)  71.9 us
    reduce_sum x1, other arithmetic, local(): select = jnp.sum(hits, axis=1).astype(jnp.bfloat16)  56.2 us
    dot_general x1, matrix products, local(): composed = jnp.dot(select, piece, preferred_element_type=jnp.float32)  29.6 us
    all_to_all x1, blocking collectives, local(): traded = lax.all_to_all(act, 'hid', split_axis=0, concat_axis=1, tiled=True)  28.5 us
    dot_general x1, matrix products, local(): jnp.dot(fingerprints, w_first, preferred_element_type=jnp.float32)  25.4 us
  transfers between devices with their start and end apart: 1, of which 1 were waited for; matrix products, arithmetic and copies ran while one was open for 24% of the time, Pallas kernels for 0%

profile of v1, /device:TPU:0, one launch (start us, length us, event | category | flops | bytes accessed | tf_op | source)
XLA Modules:
  0.0 231.5 jit_solution(13666761478747644684)
XLA Ops:
  6.5 0.0 copy-start.2
  6.5 0.0 copy-start
  6.5 0.0 copy-start.1
  6.5 0.0 all-gather.2.cloned.1.call-start
  6.5 25.4 %convolution_convert_fusion = bf16[1024,512]{1,0:T(8,128)(2,1)} fusion(bf16[1024,16384]{1,0:T(8,128)(2,1)} %param.9, bf16[16384,512]{1,0:T(8,128)(2,1)} %param.10), kind=kOutput, calls=%fused_computation.17 | convolution fusion | flops 17180393472 | bytes 51380224 | tf_op jit(solution)/shard_map/dot_general | solution.py:20
  31.9 0.0 all-gather.2.cloned.1.call-update
  32.0 0.0 copy-done.2
  32.0 0.0 copy-done
  32.0 0.0 copy-done.1
  32.0 0.0 copy-start.6
  32.1 56.2 %select_reduce_fusion = s32[2048,8192]{1,0:T(8,128)} fusion(s32[2048,3]{0,1:T(4,128)S(1)} %concatenate.4, s32[2048,3]{0,1:T(4,128)S(1)} %multiply_add_fusion.2), kind=kLoop, calls=%fused_computation | loop fusion | flops 134217728 | bytes 67158016 | tf_op jit(solution)/shard_map/reduce_sum | solution.py:29
  88.3 71.9 %all-gather.2.cloned.1.call-done = bf16[8192,512]{1,0:T(8,128)(2,1)} async-done(((bf16[1024,512]{1,0:T(8,128)(2,1)}), bf16[8192,512]{1,0:T(8,128)(2,1)}) %all-gather.2.cloned.1.call-update) | async-done | bytes 8388624 | tf_op jit(solution)/shard_map/all_gather | solution.py:26
  160.2 0.0 copy-done.6
  160.2 29.6 %fusion.6 = bf16[2048,512]{1,0:T(8,128)(2,1)} fusion(bf16[8192,512]{1,0:T(8,128)(2,1)} %all-gather.2.cloned.1.call-done, s32[2048,8192]{1,0:T(8,128)} %select_reduce_fusion, f32[512]{0:T(512)S(1)} %copy-done.6), kind=kOutput, calls=%fused_computation.9 | convolution fusion | flops 17207132160 | bytes 77596672 | tf_op jit(solution)/shard_map/dot_general | solution.py:30
  189.7 0.0 copy-start.4
  189.8 0.0 copy-start.5
  189.8 2.8 %copy.14 = bf16[4,512,512]{1,2,0:T(8,128)(2,1)S(1)} copy(bf16[4,512,512]{2,1,0:T(8,128)(2,1)} %bitcast.10) | data formatting | bytes 4194304 | tf_op jit(solution)/shard_map/all_to_all | solution.py:32
  192.6 0.0 copy-start.3
  192.6 28.5 %all_to_all.19 = bf16[4,512,512]{1,2,0:T(8,128)(2,1)S(1)} all-to-all(bf16[4,512,512]{1,2,0:T(8,128)(2,1)S(1)} %copy.14), channel_id=1, replica_groups=mesh['prod'=8,'hid'=4] {'hid'}, dimensions={0} | all-to-all | bytes 4194304 | tf_op jit(solution)/shard_map/all_to_all | solution.py:32
  221.1 0.0 copy-done.4
  221.1 0.0 copy-done.5
  221.1 0.0 copy-done.3
  221.1 3.6 %fusion.14 = f32[512]{0:T(512)} fusion(bf16[512,2048]{0,1:T(8,128)(2,1)S(1)} %bitcast.11, bf16[2048,1024]{1,0:T(8,128)(2,1)S(1)} %copy-done.3, f32[1024]{0:T(1024)S(1)} %copy-done.4, f32[1024]{0:T(1024)S(1)} %copy-done.5), kind=kOutput, calls=%fused_computation.16 | convolution fusion | flops 2153250304 | bytes 6301696 | tf_op jit(solution)/shard_map/dot_general | solution.py:33
  (2 shorter events, 0.0 us)
Async XLA Ops:
  6.5 25.4 %copy-start.2 = (s32[2048]{0:T(1024)S(1)}, s32[2048]{0:T(1024)}, u32[]{:S(2)}) copy-start(s32[2048]{0:T(1024)} %param.17) | copy-start | bytes 24580
  6.5 25.5 %copy-start = (s32[2048,3]{0,1:T(4,128)S(1)}, s32[2048,3]{0,1:T(4,128)}, u32[]{:S(2)}) copy-start(s32[2048,3]{0,1:T(4,128)} %param.16) | copy-start | bytes 73732
  6.5 25.5 %copy-start.1 = (s32[2048,3]{0,1:T(4,128)S(1)}, s32[2048,3]{0,1:T(4,128)}, u32[]{:S(2)}) copy-start(s32[2048,3]{0,1:T(4,128)} %param.15) | copy-start | bytes 73732
  6.5 153.6 %all-gather.2.cloned.1.call-start = ((), (), s32[]{:S(2)}) async-start(), calls=%async_computation.1 | async-start | bytes 9437184 | tf_op jit(solution)/shard_map/all_gather | solution.py:26
  32.0 128.1 %copy-start.6 = (f32[512]{0:T(512)S(1)}, f32[512]{0:T(512)}, u32[]{:S(2)}) copy-start(f32[512]{0:T(512)} %param.11) | copy-start | bytes 6148
  189.7 31.3 %copy-start.4 = (f32[1024]{0:T(1024)S(1)}, f32[1024]{0:T(1024)}, u32[]{:S(2)}) copy-start(f32[1024]{0:T(1024)} %param.14) | copy-start | bytes 12292
  189.8 31.3 %copy-start.5 = (f32[1024]{0:T(1024)S(1)}, f32[1024]{0:T(1024)}, u32[]{:S(2)}) copy-start(f32[1024]{0:T(1024)} %param.13) | copy-start | bytes 12292
  192.6 28.5 %copy-start.3 = (bf16[2048,1024]{1,0:T(8,128)(2,1)S(1)}, bf16[2048,1024]{1,0:T(8,128)(2,1)}, u32[]{:S(2)}) copy-start(bf16[2048,1024]{1,0:T(8,128)(2,1)} %param.12) | copy-start | bytes 12582916
Sparse Core Ops, SparseCore 0:
  32.1 128.0 all-gather.1

commit v2 on v1

v2 whole, which is shorter than its diff:
```python
import functools

import jax
import jax.numpy as jnp
from jax import lax
from jax.experimental import pallas as pl
from jax.experimental.pallas import tpu as pltpu
from jax.sharding import PartitionSpec as P

CHUNKS = 4
SLICES = 4
BUFFERS = 4
TILE = 16


def gelu_tanh(value):
    return (
        0.5
        * value
        * (1.0 + jnp.tanh(0.7978845608028654 * (value + 0.044715 * value * value * value)))
    )


def offsets(size):
    out = [(0, 0)]
    for far in range(1, size):
        out += [(far, far), (far, -far)]
    return out


def spread_kernel(nz, ny, fp_ref, w_ref, out_ref, w_all, fp_buf, acc, own, w_sem, fp_sem, own_sem, send_sem, recv_sem):
    me = lax.axis_index("prod")
    z, y = me // ny, me % ny
    rows = own.shape[0]
    step = rows // CHUNKS
    depth = w_ref.shape[0] // SLICES
    total = CHUNKS * SLICES

    def w_copy(k):
        part = pl.ds(pl.multiple_of(k * depth, depth), depth)
        return pltpu.make_async_copy(w_ref.at[part, :], w_all.at[part, :], w_sem.at[k])

    def fp_copy(s):
        slot = s % BUFFERS
        return pltpu.make_async_copy(
            fp_ref.at[
                pl.ds(pl.multiple_of((s // SLICES) * step, step), step),
                pl.ds(pl.multiple_of((s % SLICES) * depth, depth), depth),
            ],
            fp_buf.at[slot],
            fp_sem.at[slot],
        )

    for k in range(SLICES):
        w_copy(k).start()
        fp_copy(k).start()

    ways = (
        (z + 1 < nz, me + ny),
        (z >= 1, me - ny),
        (y + 1 < ny, me + 1),
        (y >= 1, me - 1),
    )
    barrier = pltpu.get_barrier_semaphore()
    count = jnp.int32(0)
    for there, target in ways:
        count = count + there.astype(jnp.int32)

        @pl.when(there)
        def _():
            pl.semaphore_signal(
                barrier, inc=1, device_id={"prod": target}, device_id_type=pl.DeviceIdType.MESH
            )

    pl.semaphore_wait(barrier, count)

    def place(src, c):
        return pl.ds(pl.multiple_of(src * rows + c * step, step), step)

    def send(c, zs, ys, mine, act):
        src = zs * ny + ys
        late = c == CHUNKS - 1
        in_col, in_row = y == ys, z == zs
        go_z = jnp.logical_or(in_col, late)
        go_y = jnp.logical_or(in_row, jnp.logical_not(late))
        want = (
            jnp.logical_and(go_z, z >= zs),
            jnp.logical_and(go_z, z <= zs),
            jnp.logical_and(go_y, y >= ys),
            jnp.logical_and(go_y, y <= ys),
        )
        for way, ((there, target), wish) in enumerate(zip(ways, want)):

            @pl.when(jnp.logical_and(there, wish))
            def _():
                source = (
                    own.at[pl.ds(pl.multiple_of(c * step, step), step), :]
                    if mine
                    else out_ref.at[place(src, c), :]
                )
                copy = pltpu.make_async_remote_copy(
                    src_ref=source,
                    dst_ref=out_ref.at[place(src, c), :],
                    send_sem=send_sem.at[way, src, c],
                    recv_sem=recv_sem.at[src, c],
                    device_id={"prod": target},
                    device_id_type=pl.DeviceIdType.MESH,
                )
                if act:
                    copy.start()
                else:
                    copy.wait_send()

    def keep(t):
        part = pl.ds(pl.multiple_of(t * step, step), step)
        return pltpu.make_async_copy(own.at[part, :], out_ref.at[place(me, t), :], own_sem.at[t])

    def compute(t, carry):
        def one(k, carry):
            s = t * SLICES + k

            @pl.when(t == 0)
            def _():
                w_copy(k).wait()

            fp_copy(s).wait()
            part = pl.ds(pl.multiple_of(k * depth, depth), depth)
            term = jnp.dot(fp_buf[s % BUFFERS], w_all[part, :], preferred_element_type=jnp.float32)

            @pl.when(k == 0)
            def _():
                acc[...] = term

            @pl.when(k > 0)
            def _():
                acc[...] += term

            @pl.when(s + BUFFERS < total)
            def _():
                fp_copy(s + BUFFERS).start()

            return carry

        lax.fori_loop(0, SLICES, one, 0)
        own[pl.ds(pl.multiple_of(t * step, step), step), :] = acc[...].astype(jnp.bfloat16)
        send(t, z, y, True, True)
        keep(t).start()
        return carry

    apart = [
        (dz, dy, far_z + far_y)
        for (far_z, dz) in offsets(nz)
        for (far_y, dy) in offsets(ny)
        if far_z + far_y > 0
    ]
    apart.sort(key=lambda item: item[2])
    furthest = apart[-1][2]

    def visit(c, act, dz, dy):
        zs, ys = z + dz, y + dy
        inside = (zs >= 0) & (zs < nz) & (ys >= 0) & (ys < ny) & (c >= 0) & (c < CHUNKS)

        @pl.when(inside)
        def _():
            if act:
                src = zs * ny + ys
                pltpu.make_async_copy(
                    out_ref.at[place(src, c), :], out_ref.at[place(src, c), :], recv_sem.at[src, c]
                ).wait()
            send(c, zs, ys, False, act)

    def turn(r, carry):
        for dz, dy, far in apart:
            visit(r - (far - 1), True, dz, dy)
        return carry

    lax.fori_loop(0, 2, compute, 0)
    turn(0, 0)
    lax.fori_loop(2, CHUNKS, compute, 0)
    lax.fori_loop(1, CHUNKS + furthest - 1, turn, 0)

    def finish(c, carry):
        send(c, z, y, True, False)
        keep(c).wait()
        for dz, dy, _ in apart:
            visit(c, False, dz, dy)
        return carry

    lax.fori_loop(0, CHUNKS, finish, 0)


def spread(fingerprints, w_first, prod):
    rows, depth = fingerprints.shape
    units = w_first.shape[1]
    nz = 4 if prod % 4 == 0 else 1
    ny = prod // nz
    return pl.pallas_call(
        functools.partial(spread_kernel, nz, ny),
        out_shape=jax.ShapeDtypeStruct((rows * prod, units), jnp.bfloat16),
        in_specs=[pl.BlockSpec(memory_space=pl.ANY)] * 2,
        out_specs=pl.BlockSpec(memory_space=pl.ANY),
        scratch_shapes=[
            pltpu.VMEM((depth, units), jnp.bfloat16),
            pltpu.VMEM((BUFFERS, rows // CHUNKS, depth // SLICES), jnp.bfloat16),
            pltpu.VMEM((rows // CHUNKS, units), jnp.float32),
            pltpu.VMEM((rows, units), jnp.bfloat16),
            pltpu.SemaphoreType.DMA((SLICES,)),
            pltpu.SemaphoreType.DMA((BUFFERS,)),
            pltpu.SemaphoreType.DMA((CHUNKS,)),
            pltpu.SemaphoreType.DMA((4, prod, CHUNKS)),
            pltpu.SemaphoreType.DMA((prod, CHUNKS)),
        ],
        compiler_params=pltpu.CompilerParams(
            collective_id=0, has_side_effects=True, vmem_limit_bytes=48 << 20
        ),
        cost_estimate=pl.CostEstimate(
            flops=2 * rows * depth * units,
            bytes_accessed=2 * (rows * depth + depth * units + rows * prod * units),
            transcendentals=0,
        ),
    )(fingerprints, w_first)


def pick_kernel(idx_ref, piece_ref, bias_ref, act_ref, table, land, group, sem):
    count = piece_ref.shape[0]
    step = land.shape[1]
    prods = act_ref.shape[0]
    steps = count // step

    def fetch(s):
        return pltpu.make_async_copy(
            piece_ref.at[pl.ds(pl.multiple_of(s * step, step), step), :],
            land.at[s % 4],
            sem.at[s % 4],
        )

    for s in range(4):
        fetch(s).start()
    table[count:, :] = jnp.zeros((table.shape[0] - count, table.shape[1]), jnp.float32)

    def widen(s, carry):
        fetch(s).wait()
        table[pl.ds(pl.multiple_of(s * step, step), step), :] = land[s % 4].astype(jnp.float32)

        @pl.when(s + 4 < steps)
        def _():
            fetch(s + 4).start()

        return carry

    lax.fori_loop(0, steps, widen, 0)
    bias = bias_ref[...]

    def some(i, carry):
        for j in range(TILE):
            p = i * TILE + j
            row = table[pl.ds(idx_ref[p], 1), :] + table[pl.ds(idx_ref[prods + p], 1), :]
            group[pl.ds(j, 1), :] = row + table[pl.ds(idx_ref[2 * prods + p], 1), :]
        act_ref[pl.ds(pl.multiple_of(i * TILE, TILE), TILE), :] = gelu_tanh(
            group[...] + bias
        ).astype(jnp.bfloat16)
        return carry

    lax.fori_loop(0, prods // TILE, some, 0)


def pick(idx, piece, bias):
    prods = idx.shape[0] // 3
    count, units = piece.shape
    step = min(512, count // 4)
    return pl.pallas_call(
        pick_kernel,
        out_shape=jax.ShapeDtypeStruct((prods, units), jnp.bfloat16),
        in_specs=[
            pl.BlockSpec(memory_space=pltpu.SMEM),
            pl.BlockSpec(memory_space=pl.ANY),
            pl.BlockSpec(memory_space=pltpu.VMEM),
        ],
        out_specs=pl.BlockSpec(memory_space=pltpu.VMEM),
        scratch_shapes=[
            pltpu.VMEM((count + 8, units), jnp.float32),
            pltpu.VMEM((4, step, units), jnp.bfloat16),
            pltpu.VMEM((TILE, units), jnp.float32),
            pltpu.SemaphoreType.DMA((4,)),
        ],
        compiler_params=pltpu.CompilerParams(vmem_limit_bytes=48 << 20),
    )(idx, piece, bias)


def local(
    prod, fingerprints, w_first, b_first, w_second, b_second, w_third, synth_block, synth_row, third_used
):
    syn_rows = fingerprints.shape[0]
    piece = spread(fingerprints, w_first, prod)
    glob = synth_block * syn_rows + synth_row
    third = jnp.where(third_used > 0, glob[:, 2], syn_rows * prod)
    idx = jnp.concatenate([glob[:, 0], glob[:, 1], third])
    act = pick(idx, piece, b_first[None, :])
    traded = lax.all_to_all(act, "hid", split_axis=0, concat_axis=1, tiled=True)
    second = jnp.dot(traded, w_second, preferred_element_type=jnp.float32)
    out = gelu_tanh(second + b_second[None, :])
    return jnp.sum(out * w_third[None, :], axis=1)


def solution(mesh):
    placed = (
        P("prod", None),
        P(None, "hid"),
        P("hid"),
        P(),
        P(),
        P(),
        P("prod", None),
        P("prod", None),
        P("prod"),
    )
    return jax.shard_map(
        functools.partial(local, mesh.shape["prod"]),
        mesh=mesh,
        in_specs=placed,
        out_specs=P(("prod", "hid")),
        check_vma=False,
    )
```

time: 232 us -> 160 us (0.69)
  Pallas kernels: 0 us -> 123 us
  waiting for transfers between devices: 72 us -> 0 us
  matrix products: 58.5 us -> 3.57 us
  other arithmetic: 56.2 us -> 1.49 us
  between operations: 13.5 us -> 0.07 us
    pallas_call x0 -> x2, Pallas kernels: none -> 123 us  [the longest x1 103 us: spread(): pl.pallas_call(functools.partial(spread_kernel, nz, ny), out_shape=jax.Sh...]
    all_gather x1 -> x0, waiting for transfers between devices: 71.9 us -> none  [local(): piece = lax.all_gather(synth_hidden, 'prod', axis=0, tiled=True)]
    reduce_sum x1 -> x0, other arithmetic: 56.2 us -> none  [local(): select = jnp.sum(hits, axis=1).astype(jnp.bfloat16)]
    dot_general x2 -> x0, matrix products: 55 us -> none  [the longest x1 29.6 us: local(): composed = jnp.dot(select, piece, preferred_element_type=jnp.float32)]
  transfers between devices with their start and end apart: 1 -> 0, of which waited for: 1 -> 0; matrix products, arithmetic and copies ran while one was open for 24% -> 0% of each run, Pallas kernels for 0% -> 0%
where the time goes in v2:
time: 160 us
  Pallas kernels  123 us (77%)
  blocking collectives  29.5 us (18%)
  matrix products  3.57 us (2%)
  local copies, waits for them, and re-layouts  2.41 us (2%)
    pallas_call x1, Pallas kernels, spread(): pl.pallas_call(functools.partial(spread_kernel, nz, ny), out_shape=jax.Sh...  103 us
    all_to_all x1, blocking collectives, local(): traded = lax.all_to_all(act, 'hid', split_axis=0, concat_axis=1, tiled=True)  29.5 us
    pallas_call x1, Pallas kernels, pick(): pl.pallas_call(pick_kernel, out_shape=jax.ShapeDtypeStruct((prods, units)...  20.2 us
    dot_general x1, matrix products, local(): second = jnp.dot(traded, w_second, preferred_element_type=jnp.float32)  3.57 us

profile of v2, /device:TPU:0, one launch (start us, length us, event | category | flops | bytes accessed | tf_op | source)
XLA Modules:
  0.0 160.1 jit_solution(3333825186358989915)
XLA Ops:
  0.0 0.8 multiply_add_fusion.1
  0.8 0.7 compare_select_fusion
  1.5 0.0 copy-start
  1.5 102.7 %shard_map.91.piece_ref = bf16[8192,512]{1,0:T(8,128)(2,1)} custom-call(bf16[1024,16384]{1,0:T(8,128)(2,1)} %fp_ref.1, bf16[16384,512]{1,0:T(8,128)(2,1)} %w_ref.1), custom_call_target="tpu_custom_call" | custom-call | flops 17179869184 | bytes 58720256 | tf_op jit(solution)/shard_map/pallas_call | solution.py:197
  104.3 0.0 copy-done
  104.3 20.2 %shard_map.92 = bf16[2048,512]{1,0:T(8,128)(2,1)S(1)} custom-call(s32[6144]{0:T(1024)S(1)} %pad_add_fusion.idx_ref, bf16[8192,512]{1,0:T(8,128)(2,1)} %shard_map.91.piece_ref, f32[1,512]{1,0:T(1,128)S(1)} %bitcast.11), custom_call_target="tpu_custom_call" | custom-call | tf_op jit(solution)/shard_map/pallas_call | solution.py:271
  124.5 0.0 copy-start.2
  124.6 0.0 copy-start.3
  124.6 2.4 %copy.10 = bf16[4,512,512]{1,2,0:T(8,128)(2,1)} copy(bf16[4,512,512]{2,1,0:T(8,128)(2,1)S(1)} %bitcast.10) | data formatting | bytes 4194304 | tf_op jit(solution)/shard_map/all_to_all | solution.py:299
  126.9 0.0 copy-start.1
  126.9 29.5 %all_to_all.19 = bf16[4,512,512]{1,2,0:T(8,128)(2,1)S(1)} all-to-all(bf16[4,512,512]{1,2,0:T(8,128)(2,1)} %copy.10), channel_id=1, replica_groups=mesh['prod'=8,'hid'=4] {'hid'}, dimensions={0} | all-to-all | bytes 4194304 | tf_op jit(solution)/shard_map/all_to_all | solution.py:299
  156.5 0.0 copy-done.2
  156.5 0.0 copy-done.3
  156.5 0.0 copy-done.1
  156.5 3.6 %fusion.5 = f32[512]{0:T(512)} fusion(bf16[512,2048]{0,1:T(8,128)(2,1)S(1)} %bitcast.12, bf16[2048,1024]{1,0:T(8,128)(2,1)S(1)} %copy-done.1, f32[1024]{0:T(1024)S(1)} %copy-done.2, f32[1024]{0:T(1024)S(1)} %copy-done.3), kind=kOutput, calls=%fused_computation.6 | convolution fusion | flops 2153250304 | bytes 6301696 | tf_op jit(solution)/shard_map/dot_general | solution.py:300
  (2 shorter events, 0.0 us)
Async XLA Ops:
  1.5 102.8 %copy-start = (f32[512]{0:T(512)S(1)}, f32[512]{0:T(512)}, u32[]{:S(2)}) copy-start(f32[512]{0:T(512)} %param.11) | copy-start | bytes 6148
  124.5 31.9 %copy-start.2 = (f32[1024]{0:T(1024)S(1)}, f32[1024]{0:T(1024)}, u32[]{:S(2)}) copy-start(f32[1024]{0:T(1024)} %param.14) | copy-start | bytes 12292
  124.6 31.9 %copy-start.3 = (f32[1024]{0:T(1024)S(1)}, f32[1024]{0:T(1024)}, u32[]{:S(2)}) copy-start(f32[1024]{0:T(1024)} %param.13) | copy-start | bytes 12292
  126.9 29.5 %copy-start.1 = (bf16[2048,1024]{1,0:T(8,128)(2,1)S(1)}, bf16[2048,1024]{1,0:T(8,128)(2,1)}, u32[]{:S(2)}) copy-start(bf16[2048,1024]{1,0:T(8,128)(2,1)} %param.12) | copy-start | bytes 12582916

commit v3 on v2

--- a/solution.py
+++ b/solution.py
@@ -11,6 +11,7 @@
 SLICES = 4
 BUFFERS = 4
 TILE = 16
+PARTS = 4
 
 
 def gelu_tanh(value):
@@ -221,10 +222,16 @@
     )(fingerprints, w_first)
 
 
-def pick_kernel(idx_ref, piece_ref, bias_ref, act_ref, table, land, group, sem):
+def pick_kernel(
+    hid, idx_ref, piece_ref, bias_ref, w_ref, b_ref, out_w_ref, score_ref, table, land, group, act, got, total, sem, send_sem, recv_sem
+):
+    me = lax.axis_index("hid")
+    chips = hid // 2
     count = piece_ref.shape[0]
     step = land.shape[1]
-    prods = act_ref.shape[0]
+    prods, units = act.shape
+    share = prods // hid
+    part = share // PARTS
     steps = count // step
 
     def fetch(s):
@@ -236,7 +243,12 @@
 
     for s in range(4):
         fetch(s).start()
-    table[count:, :] = jnp.zeros((table.shape[0] - count, table.shape[1]), jnp.float32)
+    barrier = pltpu.get_barrier_semaphore()
+    for j in range(1, hid):
+        pl.semaphore_signal(
+            barrier, inc=1, device_id={"hid": (me + j) % hid}, device_id_type=pl.DeviceIdType.MESH
+        )
+    table[count:, :] = jnp.zeros((table.shape[0] - count, units), jnp.float32)
 
     def widen(s, carry):
         fetch(s).wait()
@@ -249,57 +261,121 @@
         return carry
 
     lax.fori_loop(0, steps, widen, 0)
+    pl.semaphore_wait(barrier, hid - 1)
     bias = bias_ref[...]
 
-    def some(i, carry):
-        for j in range(TILE):
-            p = i * TILE + j
-            row = table[pl.ds(idx_ref[p], 1), :] + table[pl.ds(idx_ref[prods + p], 1), :]
-            group[pl.ds(j, 1), :] = row + table[pl.ds(idx_ref[2 * prods + p], 1), :]
-        act_ref[pl.ds(pl.multiple_of(i * TILE, TILE), TILE), :] = gelu_tanh(
-            group[...] + bias
-        ).astype(jnp.bfloat16)
-        return carry
-
-    lax.fori_loop(0, prods // TILE, some, 0)
-
-
-def pick(idx, piece, bias):
+    def target(d):
+        chip = (me // 2 + d // 2 + 1) % chips
+        return chip * 2 + (me % 2 + 1 + d) % 2
+
+    def send(dest, c):
+        return pltpu.make_async_remote_copy(
+            src_ref=act.at[pl.ds(pl.multiple_of(dest * share + c * part, part), part), :],
+            dst_ref=got.at[me, pl.ds(pl.multiple_of(c * part, part), part), :],
+            send_sem=send_sem.at[dest, c],
+            recv_sem=recv_sem.at[me, c],
+            device_id={"hid": dest},
+            device_id_type=pl.DeviceIdType.MESH,
+        )
+
+    def block(n, carry):
+        dest, c = target(n // PARTS), n % PARTS
+        first = dest * share + c * part
+
+        def some(i, carry):
+            base = first + i * TILE
+            for j in range(TILE):
+                p = base + j
+                row = table[pl.ds(idx_ref[p], 1), :] + table[pl.ds(idx_ref[prods + p], 1), :]
+                group[pl.ds(j, 1), :] = row + table[pl.ds(idx_ref[2 * prods + p], 1), :]
+            act[pl.ds(pl.multiple_of(base, TILE), TILE), :] = gelu_tanh(group[...] + bias).astype(
+                jnp.bfloat16
+            )
+            return carry
+
+        lax.fori_loop(0, part // TILE, some, 0)
+
+        @pl.when(dest != me)
+        def _():
+            send(dest, c).start()
+
+        return carry
+
+    lax.fori_loop(0, hid * PARTS, block, 0)
+
+    def weights(source):
+        return w_ref[pl.ds(pl.multiple_of(source * units, units), units), :]
+
+    mine = act[pl.ds(pl.multiple_of(me * share, share), share), :]
+    total[...] = jnp.dot(mine, weights(me), preferred_element_type=jnp.float32)
+
+    def add(d, carry):
+        source = target((d + hid - 2) % hid)
+        for c in range(PARTS):
+            pltpu.make_async_copy(
+                got.at[source, pl.ds(c * part, part), :],
+                got.at[source, pl.ds(c * part, part), :],
+                recv_sem.at[source, c],
+            ).wait()
+        total[...] += jnp.dot(got[source], weights(source), preferred_element_type=jnp.float32)
+        return carry
+
+    add(0, 0)
+    lax.fori_loop(2, hid, add, 0)
+    last = gelu_tanh(total[...] + b_ref[...]) * out_w_ref[...]
+    score_ref[...] = jnp.sum(last, axis=1, keepdims=True)
+
+    def done(n, carry):
+        send(target(n // PARTS), n % PARTS).wait_send()
+        return carry
+
+    lax.fori_loop(0, (hid - 1) * PARTS, done, 0)
+
+
+def pick(hid, idx, piece, bias, w_second, b_second, w_third):
     prods = idx.shape[0] // 3
     count, units = piece.shape
+    wide = w_second.shape[1]
+    share = prods // hid
     step = min(512, count // 4)
     return pl.pallas_call(
-        pick_kernel,
-        out_shape=jax.ShapeDtypeStruct((prods, units), jnp.bfloat16),
+        functools.partial(pick_kernel, hid),
+        out_shape=jax.ShapeDtypeStruct((share, 1), jnp.float32),
         in_specs=[
             pl.BlockSpec(memory_space=pltpu.SMEM),
             pl.BlockSpec(memory_space=pl.ANY),
-            pl.BlockSpec(memory_space=pltpu.VMEM),
-        ],
+        ]
+        + [pl.BlockSpec(memory_space=pltpu.VMEM)] * 4,
         out_specs=pl.BlockSpec(memory_space=pltpu.VMEM),
         scratch_shapes=[
             pltpu.VMEM((count + 8, units), jnp.float32),
             pltpu.VMEM((4, step, units), jnp.bfloat16),
             pltpu.VMEM((TILE, units), jnp.float32),
+            pltpu.VMEM((prods, units), jnp.bfloat16),
+            pltpu.VMEM((hid, share, units), jnp.bfloat16),
+            pltpu.VMEM((share, wide), jnp.float32),
             pltpu.SemaphoreType.DMA((4,)),
+            pltpu.SemaphoreType.DMA((hid, PARTS)),
+            pltpu.SemaphoreType.DMA((hid, PARTS)),
         ],
-        compiler_params=pltpu.CompilerParams(vmem_limit_bytes=48 << 20),
-    )(idx, piece, bias)
+        compiler_params=pltpu.CompilerParams(
+            collective_id=1, has_side_effects=True, vmem_limit_bytes=48 << 20
+        ),
+    )(idx, piece, bias, w_second, b_second, w_third)
 
 
 def local(
-    prod, fingerprints, w_first, b_first, w_second, b_second, w_third, synth_block, synth_row, third_used
+    prod, hid, fingerprints, w_first, b_first, w_second, b_second, w_third, synth_block, synth_row, third_used
 ):
     syn_rows = fingerprints.shape[0]
     piece = spread(fingerprints, w_first, prod)
     glob = synth_block * syn_rows + synth_row
     third = jnp.where(third_used > 0, glob[:, 2], syn_rows * prod)
     idx = jnp.concatenate([glob[:, 0], glob[:, 1], third])
-    act = pick(idx, piece, b_first[None, :])
-    traded = lax.all_to_all(act, "hid", split_axis=0, concat_axis=1, tiled=True)
-    second = jnp.dot(traded, w_second, preferred_element_type=jnp.float32)
-    out = gelu_tanh(second + b_second[None, :])
-    return jnp.sum(out * w_third[None, :], axis=1)
+    score = pick(
+        hid, idx, piece, b_first[None, :], w_second, b_second[None, :], w_third[None, :]
+    )
+    return score.reshape(-1)
 
 
 def solution(mesh):
@@ -315,7 +391,7 @@
         P("prod"),
     )
     return jax.shard_map(
-        functools.partial(local, mesh.shape["prod"]),
+        functools.partial(local, mesh.shape["prod"], mesh.shape["hid"]),
         mesh=mesh,
         in_specs=placed,
         out_specs=P(("prod", "hid")),

time: 160 us -> 138 us (0.86)
  blocking collectives: 29.5 us -> 0 us
  Pallas kernels: 123 us -> 135 us
  matrix products: 3.57 us -> 0 us
  local copies, waits for them, and re-layouts: 2.41 us -> 0.04 us
    all_to_all x1 -> x0, blocking collectives: 29.5 us -> none  [local(): traded = lax.all_to_all(act, 'hid', split_axis=0, concat_axis=1, tiled=True)]
    pallas_call x1, Pallas kernels: 20.2 us -> 32.6 us  [pick(): pl.pallas_call(functools.partial(pick_kernel, hid), out_shape=jax.ShapeDt...]
    dot_general x1 -> x0, matrix products: 3.57 us -> none  [local(): second = jnp.dot(traded, w_second, preferred_element_type=jnp.float32)]
    all_to_all x1 -> x0, local copies, waits for them, and re-layouts: 2.37 us -> none  [local(): traded = lax.all_to_all(act, 'hid', split_axis=0, concat_axis=1, tiled=True)]
where the time goes in v3:
time: 138 us
  Pallas kernels  135 us (98%)
  other arithmetic  2.22 us (2%)
    pallas_call x1, Pallas kernels, spread(): pl.pallas_call(functools.partial(spread_kernel, nz, ny), out_shape=jax.Sh...  103 us
    pallas_call x1, Pallas kernels, pick(): pl.pallas_call(functools.partial(pick_kernel, hid), out_shape=jax.ShapeDt...  32.6 us

profile of v3, /device:TPU:0, one launch (start us, length us, event | category | flops | bytes accessed | tf_op | source)
XLA Modules:
  0.0 137.8 jit_solution(2065667204874246657)
XLA Ops:
  0.0 0.8 multiply_add_fusion
  0.8 0.7 compare_select_fusion
  1.5 0.0 copy-start
  1.5 0.0 copy-start.1
  1.5 0.0 copy-start.2
  1.5 0.0 copy-start.3
  1.6 102.9 %shard_map.91.piece_ref = bf16[8192,512]{1,0:T(8,128)(2,1)} custom-call(bf16[1024,16384]{1,0:T(8,128)(2,1)} %fp_ref.1, bf16[16384,512]{1,0:T(8,128)(2,1)} %w_ref.2), custom_call_target="tpu_custom_call" | custom-call | flops 17179869184 | bytes 58720256 | tf_op jit(solution)/shard_map/pallas_call | solution.py:198
  104.4 0.0 copy-done
  104.4 0.0 copy-done.1
  104.4 0.0 copy-done.2
  104.4 0.0 copy-done.3
  104.5 32.6 %shard_map.92 = f32[512,1]{1,0:T(8,128)S(1)} custom-call(s32[6144]{0:T(1024)S(1)} %pad_add_fusion.idx_ref, bf16[8192,512]{1,0:T(8,128)(2,1)} %shard_map.91.piece_ref, f32[1,512]{1,0:T(1,128)S(1)} %bitcast.8, bf16[2048,1024]{1,0:T(8,128)(2,1)S(1)} %copy-done, f32[1,1024]{1,0:T(1,128)S(1)} %bitcast.6, f32[1,1024]{1,0:T(1,128)S(1)} %bitcast.7), custom_call_target="tpu_custom_call" | custom-call | tf_op jit(solution)/shard_map/pallas_call | solution.py:341
  137.0 0.7 reduce
  (2 shorter events, 0.0 us)
Async XLA Ops:
  1.5 102.9 %copy-start = (bf16[2048,1024]{1,0:T(8,128)(2,1)S(1)}, bf16[2048,1024]{1,0:T(8,128)(2,1)}, u32[]{:S(2)}) copy-start(bf16[2048,1024]{1,0:T(8,128)(2,1)} %w_ref.3) | copy-start | bytes 12582916
  1.5 102.9 %copy-start.1 = (f32[1024]{0:T(1024)S(1)}, f32[1024]{0:T(1024)}, u32[]{:S(2)}) copy-start(f32[1024]{0:T(1024)} %param.13) | copy-start | bytes 12292
  1.5 102.9 %copy-start.2 = (f32[1024]{0:T(1024)S(1)}, f32[1024]{0:T(1024)}, u32[]{:S(2)}) copy-start(f32[1024]{0:T(1024)} %param.14) | copy-start | bytes 12292
  1.5 102.9 %copy-start.3 = (f32[512]{0:T(512)S(1)}, f32[512]{0:T(512)}, u32[]{:S(2)}) copy-start(f32[512]{0:T(512)} %param.11) | copy-start | bytes 6148

commit v4 on v3

--- a/solution.py
+++ b/solution.py
@@ -7,9 +7,9 @@
 from jax.experimental.pallas import tpu as pltpu
 from jax.sharding import PartitionSpec as P
 
-CHUNKS = 4
+CHUNKS = 8
 SLICES = 4
-BUFFERS = 4
+BUFFERS = 8
 TILE = 16
 PARTS = 4
 
@@ -54,6 +54,8 @@
 
     for k in range(SLICES):
         w_copy(k).start()
+        fp_copy(k).start()
+    for k in range(SLICES, BUFFERS):
         fp_copy(k).start()
 
     ways = (
@@ -175,10 +177,12 @@
             visit(r - (far - 1), True, dz, dy)
         return carry
 
-    lax.fori_loop(0, 2, compute, 0)
-    turn(0, 0)
-    lax.fori_loop(2, CHUNKS, compute, 0)
-    lax.fori_loop(1, CHUNKS + furthest - 1, turn, 0)
+    def both(r, carry):
+        lax.fori_loop(2 * r, 2 * r + 2, compute, 0)
+        return turn(r, carry)
+
+    lax.fori_loop(0, CHUNKS // 2, both, 0)
+    lax.fori_loop(CHUNKS // 2, CHUNKS + furthest - 1, turn, 0)
 
     def finish(c, carry):
         send(c, z, y, True, False)

time: 138 us -> 144 us (1.043)
  Pallas kernels: 135 us -> 141 us
    pallas_call x1, Pallas kernels: 103 us -> 109 us  [spread(): pl.pallas_call(functools.partial(spread_kernel, nz, ny), out_shape=jax.Sh...]
where the time goes in v4:
time: 144 us
  Pallas kernels  141 us (98%)
  other arithmetic  2.22 us (2%)
    pallas_call x1, Pallas kernels, spread(): pl.pallas_call(functools.partial(spread_kernel, nz, ny), out_shape=jax.Sh...  109 us
    pallas_call x1, Pallas kernels, pick(): pl.pallas_call(functools.partial(pick_kernel, hid), out_shape=jax.ShapeDt...  32.6 us

profile of v4, /device:TPU:0, one launch (start us, length us, event | category | flops | bytes accessed | tf_op | source)
XLA Modules:
  0.0 143.6 jit_solution(8915719060245461696)
XLA Ops:
  0.0 0.8 multiply_add_fusion
  0.8 0.7 compare_select_fusion
  1.5 0.0 copy-start
  1.5 0.0 copy-start.1
  1.5 0.0 copy-start.2
  1.5 0.0 copy-start.3
  1.6 108.6 %shard_map.91.piece_ref = bf16[8192,512]{1,0:T(8,128)(2,1)} custom-call(bf16[1024,16384]{1,0:T(8,128)(2,1)} %fp_ref.1, bf16[16384,512]{1,0:T(8,128)(2,1)} %w_ref.2), custom_call_target="tpu_custom_call" | custom-call | flops 17179869184 | bytes 58720256 | tf_op jit(solution)/shard_map/pallas_call | solution.py:202
  110.2 0.0 copy-done
  110.2 0.0 copy-done.1
  110.2 0.0 copy-done.2
  110.2 0.0 copy-done.3
  110.2 32.6 %shard_map.92 = f32[512,1]{1,0:T(8,128)S(1)} custom-call(s32[6144]{0:T(1024)S(1)} %pad_add_fusion.idx_ref, bf16[8192,512]{1,0:T(8,128)(2,1)} %shard_map.91.piece_ref, f32[1,512]{1,0:T(1,128)S(1)} %bitcast.8, bf16[2048,1024]{1,0:T(8,128)(2,1)S(1)} %copy-done, f32[1,1024]{1,0:T(1,128)S(1)} %bitcast.6, f32[1,1024]{1,0:T(1,128)S(1)} %bitcast.7), custom_call_target="tpu_custom_call" | custom-call | tf_op jit(solution)/shard_map/pallas_call | solution.py:345
  142.8 0.7 reduce
  (2 shorter events, 0.0 us)
Async XLA Ops:
  1.5 108.6 %copy-start = (bf16[2048,1024]{1,0:T(8,128)(2,1)S(1)}, bf16[2048,1024]{1,0:T(8,128)(2,1)}, u32[]{:S(2)}) copy-start(bf16[2048,1024]{1,0:T(8,128)(2,1)} %w_ref.3) | copy-start | bytes 12582916
  1.5 108.6 %copy-start.1 = (f32[1024]{0:T(1024)S(1)}, f32[1024]{0:T(1024)}, u32[]{:S(2)}) copy-start(f32[1024]{0:T(1024)} %param.13) | copy-start | bytes 12292
  1.5 108.6 %copy-start.2 = (f32[1024]{0:T(1024)S(1)}, f32[1024]{0:T(1024)}, u32[]{:S(2)}) copy-start(f32[1024]{0:T(1024)} %param.14) | copy-start | bytes 12292
  1.5 108.6 %copy-start.3 = (f32[512]{0:T(512)S(1)}, f32[512]{0:T(512)}, u32[]{:S(2)}) copy-start(f32[512]{0:T(512)} %param.11) | copy-start | bytes 6148

commit v5 on v3

--- a/solution.py
+++ b/solution.py
@@ -78,12 +78,26 @@
     def place(src, c):
         return pl.ds(pl.multiple_of(src * rows + c * step, step), step)
 
+    second = step * 3 // 256 * 16
+    spans = ((0, step - second), (step - second, second))
+
+    def piece_of(start, way):
+        skip, size = spans[way]
+        return pl.ds(pl.multiple_of(start + skip, 16), size)
+
+    def arrived(src, c, order):
+        there = out_ref.at[piece_of(src * rows + c * step, order), :]
+        pltpu.make_async_copy(there, there, recv_sem.at[src, c * 2 + order]).wait()
+
     def send(c, zs, ys, mine, act):
+        send_part(c, zs, ys, mine, act, 0)
+        send_part(c, zs, ys, mine, act, 1)
+
+    def send_part(c, zs, ys, mine, act, order):
         src = zs * ny + ys
-        late = c == CHUNKS - 1
         in_col, in_row = y == ys, z == zs
-        go_z = jnp.logical_or(in_col, late)
-        go_y = jnp.logical_or(in_row, jnp.logical_not(late))
+        go_z = in_col if order == 0 else (z >= 0)
+        go_y = in_row if order == 1 else (y >= 0)
         want = (
             jnp.logical_and(go_z, z >= zs),
             jnp.logical_and(go_z, z <= zs),
@@ -95,15 +109,15 @@
             @pl.when(jnp.logical_and(there, wish))
             def _():
                 source = (
-                    own.at[pl.ds(pl.multiple_of(c * step, step), step), :]
+                    own.at[piece_of(c * step, order), :]
                     if mine
-                    else out_ref.at[place(src, c), :]
+                    else out_ref.at[piece_of(src * rows + c * step, order), :]
                 )
                 copy = pltpu.make_async_remote_copy(
                     src_ref=source,
-                    dst_ref=out_ref.at[place(src, c), :],
-                    send_sem=send_sem.at[way, src, c],
-                    recv_sem=recv_sem.at[src, c],
+                    dst_ref=out_ref.at[piece_of(src * rows + c * step, order), :],
+                    send_sem=send_sem.at[way, src, c * 2 + order],
+                    recv_sem=recv_sem.at[src, c * 2 + order],
                     device_id={"prod": target},
                     device_id_type=pl.DeviceIdType.MESH,
                 )
@@ -163,12 +177,10 @@
 
         @pl.when(inside)
         def _():
-            if act:
-                src = zs * ny + ys
-                pltpu.make_async_copy(
-                    out_ref.at[place(src, c), :], out_ref.at[place(src, c), :], recv_sem.at[src, c]
-                ).wait()
-            send(c, zs, ys, False, act)
+            for order in range(2):
+                if act:
+                    arrived(zs * ny + ys, c, order)
+                send_part(c, zs, ys, False, act, order)
 
     def turn(r, carry):
         for dz, dy, far in apart:
@@ -208,8 +220,8 @@
             pltpu.SemaphoreType.DMA((SLICES,)),
             pltpu.SemaphoreType.DMA((BUFFERS,)),
             pltpu.SemaphoreType.DMA((CHUNKS,)),
-            pltpu.SemaphoreType.DMA((4, prod, CHUNKS)),
-            pltpu.SemaphoreType.DMA((prod, CHUNKS)),
+            pltpu.SemaphoreType.DMA((4, prod, CHUNKS * 2)),
+            pltpu.SemaphoreType.DMA((prod, CHUNKS * 2)),
         ],
         compiler_params=pltpu.CompilerParams(
             collective_id=0, has_side_effects=True, vmem_limit_bytes=48 << 20

time: 138 us -> 138 us (level)
  no operation moved by 1% of the time
where the time goes in v5:
time: 138 us; the launch traced here: 137 us
  Pallas kernels  135 us (98%)
  other arithmetic  2.22 us (2%)
    pallas_call x1, Pallas kernels, spread(): pl.pallas_call(functools.partial(spread_kernel, nz, ny), out_shape=jax.Sh...  103 us
    pallas_call x1, Pallas kernels, pick(): pl.pallas_call(functools.partial(pick_kernel, hid), out_shape=jax.ShapeDt...  32.5 us

profile of v5, /device:TPU:0, one launch (start us, length us, event | category | flops | bytes accessed | tf_op | source)
XLA Modules:
  0.0 137.4 jit_solution(15729196047226512951)
XLA Ops:
  0.0 0.8 multiply_add_fusion
  0.8 0.7 compare_select_fusion
  1.5 0.0 copy-start
  1.5 0.0 copy-start.1
  1.5 0.0 copy-start.2
  1.5 0.0 copy-start.3
  1.6 102.5 %shard_map.91.piece_ref = bf16[8192,512]{1,0:T(8,128)(2,1)} custom-call(bf16[1024,16384]{1,0:T(8,128)(2,1)} %fp_ref.1, bf16[16384,512]{1,0:T(8,128)(2,1)} %w_ref.2), custom_call_target="tpu_custom_call" | custom-call | flops 17179869184 | bytes 58720256 | tf_op jit(solution)/shard_map/pallas_call | solution.py:210
  104.1 0.0 copy-done
  104.1 0.0 copy-done.1
  104.1 0.0 copy-done.2
  104.1 0.0 copy-done.3
  104.1 32.5 %shard_map.92 = f32[512,1]{1,0:T(8,128)S(1)} custom-call(s32[6144]{0:T(1024)S(1)} %pad_add_fusion.idx_ref, bf16[8192,512]{1,0:T(8,128)(2,1)} %shard_map.91.piece_ref, f32[1,512]{1,0:T(1,128)S(1)} %bitcast.8, bf16[2048,1024]{1,0:T(8,128)(2,1)S(1)} %copy-done, f32[1,1024]{1,0:T(1,128)S(1)} %bitcast.6, f32[1,1024]{1,0:T(1,128)S(1)} %bitcast.7), custom_call_target="tpu_custom_call" | custom-call | tf_op jit(solution)/shard_map/pallas_call | solution.py:353
  136.6 0.7 reduce
  (2 shorter events, 0.0 us)
Async XLA Ops:
  1.5 102.5 %copy-start = (bf16[2048,1024]{1,0:T(8,128)(2,1)S(1)}, bf16[2048,1024]{1,0:T(8,128)(2,1)}, u32[]{:S(2)}) copy-start(bf16[2048,1024]{1,0:T(8,128)(2,1)} %w_ref.3) | copy-start | bytes 12582916
  1.5 102.6 %copy-start.1 = (f32[1024]{0:T(1024)S(1)}, f32[1024]{0:T(1024)}, u32[]{:S(2)}) copy-start(f32[1024]{0:T(1024)} %param.13) | copy-start | bytes 12292
  1.5 102.6 %copy-start.2 = (f32[1024]{0:T(1024)S(1)}, f32[1024]{0:T(1024)}, u32[]{:S(2)}) copy-start(f32[1024]{0:T(1024)} %param.14) | copy-start | bytes 12292
  1.5 102.6 %copy-start.3 = (f32[512]{0:T(512)S(1)}, f32[512]{0:T(512)}, u32[]{:S(2)}) copy-start(f32[512]{0:T(512)} %param.11) | copy-start | bytes 6148

commit v6 on v5

--- a/solution.py
+++ b/solution.py
@@ -8,8 +8,8 @@
 from jax.sharding import PartitionSpec as P
 
 CHUNKS = 4
-SLICES = 4
-BUFFERS = 4
+SLICES = 8
+BUFFERS = 8
 TILE = 16
 PARTS = 4
 

time: 138 us -> 137 us (level)
  no operation moved by 1% of the time
where the time goes in v6:
time: 137 us; the launch traced here: 136 us
  Pallas kernels  134 us (98%)
  other arithmetic  2.22 us (2%)
    pallas_call x1, Pallas kernels, spread(): pl.pallas_call(functools.partial(spread_kernel, nz, ny), out_shape=jax.Sh...  102 us
    pallas_call x1, Pallas kernels, pick(): pl.pallas_call(functools.partial(pick_kernel, hid), out_shape=jax.ShapeDt...  31.8 us

profile of v6, /device:TPU:0, one launch (start us, length us, event | category | flops | bytes accessed | tf_op | source)
XLA Modules:
  0.0 136.4 jit_solution(7890589735141626916)
XLA Ops:
  0.0 0.8 multiply_add_fusion
  0.8 0.7 compare_select_fusion
  1.5 0.0 copy-start
  1.5 0.0 copy-start.1
  1.5 0.0 copy-start.2
  1.5 0.0 copy-start.3
  1.6 102.2 %shard_map.91.piece_ref = bf16[8192,512]{1,0:T(8,128)(2,1)} custom-call(bf16[1024,16384]{1,0:T(8,128)(2,1)} %fp_ref.1, bf16[16384,512]{1,0:T(8,128)(2,1)} %w_ref.2), custom_call_target="tpu_custom_call" | custom-call | flops 17179869184 | bytes 58720256 | tf_op jit(solution)/shard_map/pallas_call | solution.py:210
  103.8 0.0 copy-done
  103.8 0.0 copy-done.1
  103.8 0.0 copy-done.2
  103.8 0.0 copy-done.3
  103.8 31.8 %shard_map.92 = f32[512,1]{1,0:T(8,128)S(1)} custom-call(s32[6144]{0:T(1024)S(1)} %pad_add_fusion.idx_ref, bf16[8192,512]{1,0:T(8,128)(2,1)} %shard_map.91.piece_ref, f32[1,512]{1,0:T(1,128)S(1)} %bitcast.8, bf16[2048,1024]{1,0:T(8,128)(2,1)S(1)} %copy-done, f32[1,1024]{1,0:T(1,128)S(1)} %bitcast.6, f32[1,1024]{1,0:T(1,128)S(1)} %bitcast.7), custom_call_target="tpu_custom_call" | custom-call | tf_op jit(solution)/shard_map/pallas_call | solution.py:353
  135.7 0.7 reduce
  (2 shorter events, 0.0 us)
Async XLA Ops:
  1.5 102.2 %copy-start = (bf16[2048,1024]{1,0:T(8,128)(2,1)S(1)}, bf16[2048,1024]{1,0:T(8,128)(2,1)}, u32[]{:S(2)}) copy-start(bf16[2048,1024]{1,0:T(8,128)(2,1)} %w_ref.3) | copy-start | bytes 12582916
  1.5 102.3 %copy-start.1 = (f32[1024]{0:T(1024)S(1)}, f32[1024]{0:T(1024)}, u32[]{:S(2)}) copy-start(f32[1024]{0:T(1024)} %param.13) | copy-start | bytes 12292
  1.5 102.3 %copy-start.2 = (f32[1024]{0:T(1024)S(1)}, f32[1024]{0:T(1024)}, u32[]{:S(2)}) copy-start(f32[1024]{0:T(1024)} %param.14) | copy-start | bytes 12292
  1.5 102.3 %copy-start.3 = (f32[512]{0:T(512)S(1)}, f32[512]{0:T(512)}, u32[]{:S(2)}) copy-start(f32[512]{0:T(512)} %param.11) | copy-start | bytes 6148
